TPU v7x, 32 devices: a whole 2x2x4 slice. The times are simulated.
32 devices in a mesh: seq: 4 (over z), batch: 8 (over y, x, core).
Axes of the slice: x: 2, y: 2, z: 4, core: 2. Of those that a mesh axis runs over, the one named last changes fastest.
Arguments:
- dt_raw: float32 [8, 512, 40], P('batch', 'seq'), may hold values from -6 to 64
- dt_bias: float32 [40], replicated, may hold values from -2.5 to -1
- a_log: float32 [40], replicated, may hold values from -10 to -1
- d_skip: float32 [40], replicated, may hold values from 0.5 to 1.5
- x_in: bfloat16 [8, 512, 2560], P('batch', 'seq'), may hold values from -6 to 6
- b_in: bfloat16 [8, 512, 128], P('batch', 'seq'), may hold values from -1.796875 to 1.796875
- c_in: bfloat16 [8, 512, 128], P('batch', 'seq'), may hold values from -0.52734375 to 0.52734375
- cotangent: bfloat16 [8, 512, 2560], P('batch', 'seq'), may hold values from -6 to 6
Outputs:
- layer_out: bfloat16 [8, 512, 2560], P('batch', 'seq')
- grad_x: bfloat16 [8, 512, 2560], P('batch', 'seq')
- grad_b: bfloat16 [8, 512, 128], P('batch', 'seq')
- grad_c: bfloat16 [8, 512, 128], P('batch', 'seq')
- grad_dt_raw: float32 [8, 512, 40], P('batch', 'seq')
- grad_a_log: float32 [40], replicated
- grad_dt_bias: float32 [40], replicated
- grad_d_skip: float32 [40], replicated
All inputs are finite; a program needn't handle non-finite values.
Results may differ from a plain program's by a relative error of at most 0.024.
Values may be sent and summed in bfloat16 or wider, within the bound.
A program may use at most 64 MiB of HBM per device.

v0:
```python
import functools

import jax
import jax.numpy as jnp
from jax import lax
from jax.experimental import pallas as pl
from jax.experimental.pallas import tpu as pltpu
from jax.sharding import PartitionSpec as P

HEAD_DIM = 64
WIDTH = 256
LAG = 2
FLAT = 64
LOG2E = 1.4426950408889634
F32 = jnp.float32
BF16 = jnp.bfloat16


def mm(a, b):
    return jnp.dot(a, b, preferred_element_type=F32)


def mm_nt(a, b):
    return lax.dot_general(a, b, (((1,), (1,)), ((), ())), preferred_element_type=F32)


def exact(a, b):
    return jnp.dot(a, b, preferred_element_type=F32, precision=lax.Precision.HIGHEST)


def iota(shape, dim):
    return lax.broadcasted_iota(jnp.int32, shape, dim)


def split3(value, heads):
    high = value.astype(BF16).astype(F32)
    rest = value - high
    mid = rest.astype(BF16).astype(F32)
    low = (rest - mid).astype(BF16).astype(F32)
    packed = high + pltpu.roll(mid, heads, 1) + pltpu.roll(low, 2 * heads, 1)
    return packed.astype(BF16)


def kernel(
    n, m, heads, tokens,
    dt_ref, bias_ref, alog_ref, skip_ref, x_hbm, b_ref, c_ref, g_hbm,
    out_ref, gx_ref, gb_ref, gc_ref, gdt_ref, red_ref,
    x_ref, g_ref, in_sem, pad, prm, pk, apk, vt, kmod, cbm, ms, ee, we, wx, eg, sl, dc, vin, uin,
    fsend, car, bsend, ds,
    rowa, cola, misc, dcb, gba, gca, reds, redb,
    fs_sem, fr_sem, bs_sem, br_sem, rs_send, rs_recv, rb_send, rb_recv,
):
    z = lax.axis_index("seq")
    w = lax.axis_index("batch")
    chunks = heads * HEAD_DIM // WIDTH
    per = WIDTH // HEAD_DIM

    fetch_x = pltpu.make_async_copy(x_hbm, x_ref, in_sem.at[0])
    fetch_g = pltpu.make_async_copy(g_hbm, g_ref, in_sem.at[1])
    fetch_x.start()
    fetch_g.start()
    barrier = pltpu.get_barrier_semaphore()

    def other(d):
        place = lax.rem(z * m + w + d, n * m)
        return {"seq": lax.div(place, m), "batch": lax.rem(place, m)}

    def greet_seq(d, _):
        pl.semaphore_signal(barrier, inc=1, device_id={"seq": lax.rem(z + d, n)},
                            device_id_type=pl.DeviceIdType.MESH)
        return 0

    def greet_batch(d, _):
        pl.semaphore_signal(barrier, inc=1, device_id={"batch": lax.rem(w + d, m)},
                            device_id_type=pl.DeviceIdType.MESH)
        return 0

    def greet_all(d, _):
        pl.semaphore_signal(barrier, inc=1, device_id=other(d),
                            device_id_type=pl.DeviceIdType.MESH)
        return 0

    flat = n * m <= FLAT
    peers = n * m - 1 if flat else n + m - 2
    if flat:
        lax.fori_loop(1, n * m, greet_all, 0)
    else:
        lax.fori_loop(1, n, greet_seq, 0)
        lax.fori_loop(1, m, greet_batch, 0)

    def fcopy(i):
        return pltpu.make_async_remote_copy(
            src_ref=fsend.at[i], dst_ref=car.at[i], send_sem=fs_sem.at[i], recv_sem=fr_sem.at[i],
            device_id={"seq": jnp.minimum(z + 1, n - 1)}, device_id_type=pl.DeviceIdType.MESH)

    def bcopy(i):
        return pltpu.make_async_remote_copy(
            src_ref=bsend.at[i], dst_ref=ds.at[i], send_sem=bs_sem.at[i], recv_sem=br_sem.at[i],
            device_id={"seq": jnp.maximum(z - 1, 0)}, device_id_type=pl.DeviceIdType.MESH)

    pad[...] = jnp.zeros_like(pad)
    pad[0:heads, :] = dt_ref[...]
    prm[...] = jnp.zeros_like(prm)
    prm[0:1, :heads] = bias_ref[...]
    prm[1:2, :heads] = alog_ref[...]
    prm[2:3, :heads] = skip_ref[...]
    square = (tokens, tokens)
    is_head = iota(square, 1) < heads
    raw = pad[...].T + prm[0:1, :]
    step = jnp.maximum(raw, 0.0) + jnp.log1p(jnp.exp(-jnp.abs(raw)))
    rate = jnp.exp(prm[1:2, :])
    decay = jnp.where(is_head, -rate * step, 0.0)
    causal = iota(square, 0) >= iota(square, 1)
    cum = exact(jnp.where(causal, 1.0, 0.0), decay)
    last = cum[tokens - 1 : tokens, :]
    pk[0:tokens, :] = split3(jnp.where(is_head, jnp.exp(cum), 0.0), heads)
    pk[tokens : 2 * tokens, :] = split3(
        jnp.where(is_head, jnp.exp(last - cum) * step, 0.0), heads)
    head_row = is_head[0:1, :]
    factor = jnp.where(head_row, jnp.exp(last.astype(BF16).astype(F32)), 0.0)
    row16 = iota((16, tokens), 0)
    pk[2 * tokens : 2 * tokens + 16, :] = split3(
        jnp.where(row16 == 0, prm[2:3, :], 0.0) + jnp.where(row16 == 1, factor, 0.0), heads)
    k = iota((tokens, WIDTH), 0)
    kmod[...] = k - jnp.where(k >= heads, heads, 0) - jnp.where(k >= 2 * heads, heads, 0)
    b16 = b_ref[...]
    c16 = c_ref[...]
    bt = b16.astype(F32).T.astype(BF16)
    ct = c16.astype(F32).T.astype(BF16)

    fetch_x.wait()
    fetch_g.wait()
    pl.semaphore_wait(barrier, peers)

    def cols(i):
        return pl.ds(pl.multiple_of(i * WIDTH, WIDTH), WIDTH)

    def states(i, _):
        group = lax.shift_right_logical(iota((tokens, WIDTH), 1), 6)
        spread = jnp.where(kmod[...] - group == i * per, 1.0, 0.0).astype(BF16)
        wide = mm(pk[...], spread)
        ee[i] = wide[0:tokens]
        we[i] = wide[tokens : 2 * tokens]
        ms[i] = wide[2 * tokens : 2 * tokens + 8]
        wx_i = (x_ref[:, cols(i)].astype(F32) * wide[tokens : 2 * tokens]).astype(BF16)
        eg_i = (g_ref[:, cols(i)].astype(F32) * wide[0:tokens]).astype(BF16)
        wx[i] = wx_i
        eg[i] = eg_i
        sl_i = mm(bt, wx_i)
        dc_i = mm(ct, eg_i)
        sl[i] = sl_i
        dc[i] = dc_i

        @pl.when(z == 0)
        def _():
            car[i] = jnp.zeros((tokens, WIDTH), BF16)
            fsend[i] = sl_i.astype(BF16)
            fcopy(i).start()

        @pl.when(z == n - 1)
        def _():
            ds[i] = jnp.zeros((tokens, WIDTH), BF16)
            bsend[i] = dc_i.astype(BF16)
            bcopy(i).start()

        return 0

    lax.fori_loop(0, chunks, states, 0)

    cum2 = cum * LOG2E
    apk[...] = split3(cum2, heads)
    vt[...] = (cum2 - jnp.log(step) * LOG2E).T
    cbm[...] = jnp.where(causal, mm(c16, bt), 0.0)
    for acc in (rowa, cola, misc, dcb, gba, gca):
        acc[...] = jnp.zeros_like(acc)

    def to_heads(value, i):
        group = lax.shift_right_logical(iota((WIDTH, tokens), 0), 6)
        gather = jnp.where(iota((WIDTH, tokens), 1) - group == i * per, 1.0, 0.0).astype(BF16)
        high = value.astype(BF16)
        low = (value - high.astype(F32)).astype(BF16)
        return mm(high, gather) + mm(low, gather)

    def within(i):
        lane = iota(square, 1)
        left = jnp.where(lane < HEAD_DIM, 1.0, 0.0).astype(BF16)
        right = jnp.where(lane < HEAD_DIM, 0.0, 1.0).astype(BF16)
        second = jnp.where(iota((tokens, 2 * tokens), 1) < tokens, 0, 1)
        table = kmod[:, 0:1] - second
        cb2 = jnp.concatenate([cbm[...], cbm[...]], axis=1)
        for q in range(WIDTH // 128):
            head = i * per + 2 * q
            pair = pl.ds(pl.multiple_of(i * WIDTH + q * 128, 128), 128)
            xq = x_ref[:, pair]
            gq = g_ref[:, pair]
            xs = jnp.concatenate([xq * left, xq * right], axis=0)
            gs = jnp.concatenate([gq * left, gq * right], axis=0)
            pick = jnp.where(table == head, 1.0, 0.0).astype(BF16)
            v_row = jnp.concatenate([vt[pl.ds(head, 1), :], vt[pl.ds(head + 1, 1), :]], axis=1)
            gate = jnp.exp2(jnp.minimum(mm(apk[...], pick) - v_row, 100.0))
            scores = (gate * cb2).astype(BF16)
            vin[i, :, q * 128 : (q + 1) * 128] = mm(scores, xs)
            turned = jnp.concatenate([scores[:, :tokens].T, scores[:, tokens:].T], axis=1)
            uin[i, :, q * 128 : (q + 1) * 128] = mm(turned, gs)
            d_gate = mm_nt(gq, xs) * gate
            dcb[...] += d_gate[:, :tokens] + d_gate[:, tokens:]

    def forward(i):
        x_i = x_ref[:, cols(i)].astype(F32)
        v = vin[i] + ee[i] * mm(c16, car[i])
        out_ref[:, cols(i)] = (v + ms[i, 0:1, :] * x_i).astype(BF16)
        rowa[...] += to_heads(g_ref[:, cols(i)].astype(F32) * v, i)
        gca[...] += mm_nt(eg[i], car[i])

    def backward(i):
        g_i = g_ref[:, cols(i)].astype(F32)
        u = uin[i]
        from_state = mm(b16, ds[i])
        gx_ref[:, cols(i)] = (u + we[i] * from_state + ms[i, 0:1, :] * g_i).astype(BF16)
        share = x_ref[:, cols(i)].astype(F32) * u + wx[i].astype(F32) * from_state
        cola[...] += to_heads(share, i)
        gba[...] += mm_nt(wx[i], ds[i])

    def sums(i):
        onward = ms[i, 1:2, :] * car[i].astype(F32) + sl[i]
        d_last = jnp.sum(onward * ds[i].astype(F32), axis=0, keepdims=True)
        d_skip = jnp.sum(
            g_ref[:, cols(i)].astype(F32) * x_ref[:, cols(i)].astype(F32), axis=0, keepdims=True)
        row = iota((8, WIDTH), 0)
        both = jnp.where(row == 0, d_last, 0.0) + jnp.where(row == 1, d_skip, 0.0)
        misc[...] += to_heads(both, i)

    def advance(j, _):
        f = j - LAG * jnp.maximum(z - 1, 0)
        b = j - LAG * jnp.maximum(n - 2 - z, 0)
        both = jnp.minimum(f, b)
        f_on = (f >= 0) & (f < chunks)
        b_on = (b >= 0) & (b < chunks)

        @pl.when(f_on & (z > 0))
        def _():
            fcopy(f).wait_recv()
            fsend[f] = (ms[f, 1:2, :] * car[f].astype(F32) + sl[f]).astype(BF16)

        @pl.when(f_on & (z > 0) & (z < n - 1))
        def _():
            fcopy(f).start()

        @pl.when(b_on & (z < n - 1))
        def _():
            bcopy(b).wait_recv()

        @pl.when(b_on & (z < n - 1) & (z > 0))
        def _():
            bsend[b] = (ms[b, 1:2, :] * ds[b].astype(F32) + dc[b]).astype(BF16)
            bcopy(b).start()

        @pl.when(j < chunks)
        def _():
            within(j)

        @pl.when(f_on)
        def _():
            forward(f)

        @pl.when(b_on)
        def _():
            backward(b)

        @pl.when((both >= 0) & (both < chunks))
        def _():
            sums(both)

        return 0

    lax.fori_loop(0, chunks + LAG * max(n - 2, 0), advance, 0)

    d_cum = rowa[...] - cola[...]
    d_cum = d_cum + jnp.where(iota(square, 0) == tokens - 1, misc[0:1, :], 0.0)
    later = iota(square, 0) <= iota(square, 1)
    d_decay = exact(jnp.where(later, 1.0, 0.0), d_cum)
    d_step = cola[...] / step - rate * d_decay
    d_raw = d_step * (1.0 / (1.0 + jnp.exp(-raw)))
    row8 = iota((8, tokens), 0)
    mine = (
        jnp.where(row8 == 0, jnp.sum(d_decay * decay, axis=0, keepdims=True), 0.0)
        + jnp.where(row8 == 1, jnp.sum(d_raw, axis=0, keepdims=True), 0.0)
        + jnp.where(row8 == 2, misc[1:2, :], 0.0)
    )

    def seq_copy(d):
        return pltpu.make_async_remote_copy(
            src_ref=reds.at[z], dst_ref=reds.at[z], send_sem=rs_send.at[d - 1],
            recv_sem=rs_recv.at[d - 1], device_id={"seq": lax.rem(z + d, n)},
            device_id_type=pl.DeviceIdType.MESH)

    def batch_copy(d):
        return pltpu.make_async_remote_copy(
            src_ref=redb.at[w], dst_ref=redb.at[w], send_sem=rb_send.at[d - 1],
            recv_sem=rb_recv.at[d - 1], device_id={"batch": lax.rem(w + d, m)},
            device_id_type=pl.DeviceIdType.MESH)

    def flat_copy(d):
        place = z * m + w
        return pltpu.make_async_remote_copy(
            src_ref=redb.at[place], dst_ref=redb.at[place], send_sem=rb_send.at[d - 1],
            recv_sem=rb_recv.at[d - 1], device_id=other(d),
            device_id_type=pl.DeviceIdType.MESH)

    def start(copy):
        return lambda d, _: (copy(d).start(), 0)[1]

    def finish(copy):
        return lambda d, _: (copy(d).wait(), 0)[1]

    if flat:
        redb[z * m + w] = mine
        lax.fori_loop(1, n * m, start(flat_copy), 0)
    else:
        reds[z] = mine
        lax.fori_loop(1, n, start(seq_copy), 0)
    gdt_ref[...] = d_raw.T[0:heads, :]
    d_cb = jnp.where(causal, dcb[...], 0.0)
    gc_ref[...] = (gca[...] + mm(d_cb.astype(BF16), b16)).astype(BF16)
    gb_ref[...] = (gba[...] + mm(d_cb.T.astype(BF16), c16)).astype(BF16)
    if not flat:
        lax.fori_loop(1, n, finish(seq_copy), 0)
        redb[w] = lax.fori_loop(0, n, lambda i, t: t + reds[i], jnp.zeros((8, tokens), F32))
        lax.fori_loop(1, m, start(batch_copy), 0)

    def drain(i, _):
        @pl.when(z < n - 1)
        def _():
            fcopy(i).wait_send()

        @pl.when(z > 0)
        def _():
            bcopy(i).wait_send()

        return 0

    lax.fori_loop(0, chunks, drain, 0)
    if flat:
        lax.fori_loop(1, n * m, finish(flat_copy), 0)
    else:
        lax.fori_loop(1, m, finish(batch_copy), 0)
    red_ref[...] = jnp.sum(redb[...], axis=0)


def place_outputs(heads, out, gx, gb, gc, gdt, red, to_out, to_gx, to_gb, to_gc, to_gdt,
                  alog, bias, skip, sems):
    pairs = ((out, to_out), (gx, to_gx), (gb, to_gb), (gc, to_gc), (gdt, to_gdt))
    copies = [pltpu.make_async_copy(a, b, sems.at[i]) for i, (a, b) in enumerate(pairs)]
    for copy in copies:
        copy.start()
    alog[...] = red[0:1, :heads]
    bias[...] = red[1:2, :heads]
    skip[...] = red[2:3, :heads]
    for copy in copies:
        copy.wait()


def shards(dt_raw, dt_bias, a_log, d_skip, x_in, b_in, c_in, cotangent):
    n, m = lax.axis_size("seq"), lax.axis_size("batch")
    _, tokens, heads = dt_raw.shape
    channels = x_in.shape[2]
    state = b_in.shape[2]
    chunks = channels // WIDTH
    steps = n * m - 1 if n * m <= FLAT else m - 1
    big = (chunks, tokens, WIDTH)
    square = (tokens, tokens)
    vmem = pl.BlockSpec(memory_space=pltpu.VMEM)
    hbm = pl.BlockSpec(memory_space=pltpu.HBM)
    dma = pltpu.SemaphoreType.DMA
    shape = jax.ShapeDtypeStruct
    made = pl.pallas_call(
        functools.partial(kernel, n, m, heads, tokens),
        out_shape=(
            shape((tokens, channels), BF16),
            shape((tokens, channels), BF16),
            shape((tokens, state), BF16),
            shape((tokens, state), BF16),
            shape((heads, tokens), F32),
            shape((8, tokens), F32),
        ),
        in_specs=[vmem] * 4 + [hbm, vmem, vmem, hbm],
        out_specs=(vmem,) * 6,
        scratch_shapes=[
            pltpu.VMEM((tokens, channels), BF16),
            pltpu.VMEM((tokens, channels), BF16),
            dma((2,)),
            pltpu.VMEM(square, F32),
            pltpu.VMEM((8, tokens), F32),
            pltpu.VMEM((2 * tokens + 16, tokens), BF16),
            pltpu.VMEM(square, BF16),
            pltpu.VMEM(square, F32),
            pltpu.VMEM((tokens, WIDTH), jnp.int32),
            pltpu.VMEM(square, F32),
            pltpu.VMEM((chunks, 8, WIDTH), F32),
            pltpu.VMEM(big, F32),
            pltpu.VMEM(big, F32),
            pltpu.VMEM(big, BF16),
            pltpu.VMEM(big, BF16),
            pltpu.VMEM(big, F32),
            pltpu.VMEM(big, F32),
            pltpu.VMEM(big, F32),
            pltpu.VMEM(big, F32),
            pltpu.VMEM(big, BF16),
            pltpu.VMEM(big, BF16),
            pltpu.VMEM(big, BF16),
            pltpu.VMEM(big, BF16),
            pltpu.VMEM(square, F32),
            pltpu.VMEM(square, F32),
            pltpu.VMEM((8, tokens), F32),
            pltpu.VMEM(square, F32),
            pltpu.VMEM(square, F32),
            pltpu.VMEM(square, F32),
            pltpu.VMEM((n, 8, tokens), F32),
            pltpu.VMEM((steps + 1, 8, tokens), F32),
            dma((chunks,)), dma((chunks,)), dma((chunks,)), dma((chunks,)),
            dma((n - 1,)), dma((n - 1,)), dma((steps,)), dma((steps,)),
        ],
        compiler_params=pltpu.CompilerParams(
            collective_id=0, has_side_effects=True, vmem_limit_bytes=60 * 2**20),
    )(
        dt_raw[0].T, dt_bias[None], a_log[None], d_skip[None],
        x_in[0], b_in[0], c_in[0], cotangent[0],
    )
    out, gx, gb, gc, gdt, alog, bias, skip = pl.pallas_call(
        functools.partial(place_outputs, heads),
        out_shape=tuple(shape(a.shape, a.dtype) for a in made[:5]) + (shape((1, heads), F32),) * 3,
        in_specs=[vmem] * 6,
        out_specs=(hbm,) * 5 + (vmem,) * 3,
        scratch_shapes=[dma((5,))],
    )(*made)
    return (out[None], gx[None], gb[None], gc[None], gdt.T[None], alog[0], bias[0], skip[0])


def solution(mesh):
    rows = P("batch", "seq", None)
    return jax.shard_map(
        shards,
        mesh=mesh,
        in_specs=(rows, P(), P(), P(), rows, rows, rows, rows),
        out_specs=(rows, rows, rows, rows, rows, P(), P(), P()),
        check_vma=False,
    )
```

profile of v0, /device:TPU:0, one launch (start us, length us, event | category | flops | bytes accessed | tf_op | source)
XLA Modules:
  0.0 43.9 jit_solution(16206774642039508677)
XLA Ops:
  0.6 40.3 %shard_map.143 = (bf16[128,2560]{1,0:T(8,128)(2,1)}, bf16[128,2560]{1,0:T(8,128)(2,1)}, bf16[128,128]{1,0:T(8,128)(2,1)}, bf16[128,128]{1,0:T(8,128)(2,1)}, f32[40,128]{1,0:T(8,128)}, /*index=5*/f32[8,128]{1,0:T(8,128)}) custom-call(f32[40,128]{1,0:T(8,128)} %bitcast.24, f32[1,40]{1,0:T(1,128)} %bitcast.25, f32[1,40]{1,0:T(1,128)} %bitcast.26, ...), custom_call_target="tpu_custom_call" | custom-call | tf_op jit(solution)/shard_map/pallas_call | solution.py:376
  40.9 2.9 %shard_map.144 = (bf16[128,2560]{1,0:T(8,128)(2,1)}, bf16[128,2560]{1,0:T(8,128)(2,1)}, bf16[128,128]{1,0:T(8,128)(2,1)}, bf16[128,128]{1,0:T(8,128)(2,1)}, f32[...) custom-call(bf16[128,2560]{1,0:T(8,128)(2,1)} %get-tuple-element.22.out, ...), custom_call_target="tpu_custom_call" | custom-call | tf_op jit(solution)/shard_map/pallas_call | solution.py:429
where the time goes:
time: 44.1 us; the launch traced here: 43.9 us
  Pallas kernels  43.2 us (98%)
  between operations  0.64 us (1%)
    pallas_call x1, Pallas kernels, shards(): pl.pallas_call(functools.partial(kernel, n, m, heads, tokens), out_shape=...  40.3 us
    pallas_call x1, Pallas kernels, shards(): pl.pallas_call(functools.partial(place_outputs, heads), out_shape=tuple((...  2.93 us

commit v1 on v0

--- a/solution.py
+++ b/solution.py
@@ -9,7 +9,7 @@
 
 HEAD_DIM = 64
 WIDTH = 256
-LAG = 2
+LAG = 3
 FLAT = 64
 LOG2E = 1.4426950408889634
 F32 = jnp.float32
@@ -43,9 +43,10 @@
 
 def kernel(
     n, m, heads, tokens,
-    dt_ref, bias_ref, alog_ref, skip_ref, x_hbm, b_ref, c_ref, g_hbm,
-    out_ref, gx_ref, gb_ref, gc_ref, gdt_ref, red_ref,
-    x_ref, g_ref, in_sem, pad, prm, pk, apk, vt, kmod, cbm, ms, ee, we, wx, eg, sl, dc, vin, uin,
+    dt_hbm, bias_hbm, alog_hbm, skip_hbm, x_hbm, b_hbm, c_hbm, g_hbm,
+    out_ref, gx_ref, gb_ref, gc_ref, gdt_ref, ga_out, gbias_out, gskip_out,
+    dt_ref, bias_ref, alog_ref, skip_ref, x_ref, b_ref, c_ref, g_ref,
+    in_sem, pad, prm, pk, apk, vt, kmod, cbm, ms, ee, we, wx, eg, sl, dc, vin, uin,
     fsend, car, bsend, ds,
     rowa, cola, misc, dcb, gba, gca, reds, redb,
     fs_sem, fr_sem, bs_sem, br_sem, rs_send, rs_recv, rb_send, rb_recv,
@@ -55,10 +56,14 @@
     chunks = heads * HEAD_DIM // WIDTH
     per = WIDTH // HEAD_DIM
 
-    fetch_x = pltpu.make_async_copy(x_hbm, x_ref, in_sem.at[0])
-    fetch_g = pltpu.make_async_copy(g_hbm, g_ref, in_sem.at[1])
-    fetch_x.start()
-    fetch_g.start()
+    fetches = [
+        pltpu.make_async_copy(a, b, in_sem.at[i])
+        for i, (a, b) in enumerate((
+            (dt_hbm, dt_ref), (bias_hbm, bias_ref), (alog_hbm, alog_ref), (skip_hbm, skip_ref),
+            (b_hbm, b_ref), (c_hbm, c_ref), (x_hbm, x_ref), (g_hbm, g_ref)))
+    ]
+    for fetch in fetches:
+        fetch.start()
     barrier = pltpu.get_barrier_semaphore()
 
     def other(d):
@@ -99,8 +104,10 @@
             device_id={"seq": jnp.maximum(z - 1, 0)}, device_id_type=pl.DeviceIdType.MESH)
 
     pad[...] = jnp.zeros_like(pad)
+    prm[...] = jnp.zeros_like(prm)
+    for fetch in fetches[:6]:
+        fetch.wait()
     pad[0:heads, :] = dt_ref[...]
-    prm[...] = jnp.zeros_like(prm)
     prm[0:1, :heads] = bias_ref[...]
     prm[1:2, :heads] = alog_ref[...]
     prm[2:3, :heads] = skip_ref[...]
@@ -128,8 +135,8 @@
     bt = b16.astype(F32).T.astype(BF16)
     ct = c16.astype(F32).T.astype(BF16)
 
-    fetch_x.wait()
-    fetch_g.wait()
+    for fetch in fetches[6:]:
+        fetch.wait()
     pl.semaphore_wait(barrier, peers)
 
     def cols(i):
@@ -281,11 +288,17 @@
     d_decay = exact(jnp.where(later, 1.0, 0.0), d_cum)
     d_step = cola[...] / step - rate * d_decay
     d_raw = d_step * (1.0 / (1.0 + jnp.exp(-raw)))
-    row8 = iota((8, tokens), 0)
+
+    def turn(row, by):
+        return pltpu.roll(jnp.broadcast_to(row, (8, tokens)), by, 1)[0:1, :]
+
+    def per_head(row):
+        return jnp.where(head_row, row, 0.0)
+
     mine = (
-        jnp.where(row8 == 0, jnp.sum(d_decay * decay, axis=0, keepdims=True), 0.0)
-        + jnp.where(row8 == 1, jnp.sum(d_raw, axis=0, keepdims=True), 0.0)
-        + jnp.where(row8 == 2, misc[1:2, :], 0.0)
+        per_head(jnp.sum(d_decay * decay, axis=0, keepdims=True))
+        + turn(per_head(jnp.sum(d_raw, axis=0, keepdims=True)), heads)
+        + turn(per_head(misc[1:2, :]), 2 * heads)
     )
 
     def seq_copy(d):
@@ -325,7 +338,7 @@
     gb_ref[...] = (gba[...] + mm(d_cb.T.astype(BF16), c16)).astype(BF16)
     if not flat:
         lax.fori_loop(1, n, finish(seq_copy), 0)
-        redb[w] = lax.fori_loop(0, n, lambda i, t: t + reds[i], jnp.zeros((8, tokens), F32))
+        redb[w] = lax.fori_loop(0, n, lambda i, t: t + reds[i], jnp.zeros((1, tokens), F32))
         lax.fori_loop(1, m, start(batch_copy), 0)
 
     def drain(i, _):
@@ -344,18 +357,19 @@
         lax.fori_loop(1, n * m, finish(flat_copy), 0)
     else:
         lax.fori_loop(1, m, finish(batch_copy), 0)
-    red_ref[...] = jnp.sum(redb[...], axis=0)
-
-
-def place_outputs(heads, out, gx, gb, gc, gdt, red, to_out, to_gx, to_gb, to_gc, to_gdt,
-                  alog, bias, skip, sems):
-    pairs = ((out, to_out), (gx, to_gx), (gb, to_gb), (gc, to_gc), (gdt, to_gdt))
-    copies = [pltpu.make_async_copy(a, b, sems.at[i]) for i, (a, b) in enumerate(pairs)]
+    total = jnp.sum(redb[...], axis=0)
+    ga_out[...] = total[:, :heads]
+    gbias_out[...] = turn(total, tokens - heads)[:, :heads]
+    gskip_out[...] = turn(total, tokens - 2 * heads)[:, :heads]
+
+
+def place_outputs(count, *refs):
+    sems = refs[2 * count]
+    copies = [
+        pltpu.make_async_copy(refs[i], refs[count + i], sems.at[i]) for i in range(count)
+    ]
     for copy in copies:
         copy.start()
-    alog[...] = red[0:1, :heads]
-    bias[...] = red[1:2, :heads]
-    skip[...] = red[2:3, :heads]
     for copy in copies:
         copy.wait()
 
@@ -381,14 +395,19 @@
             shape((tokens, state), BF16),
             shape((tokens, state), BF16),
             shape((heads, tokens), F32),
-            shape((8, tokens), F32),
-        ),
-        in_specs=[vmem] * 4 + [hbm, vmem, vmem, hbm],
-        out_specs=(vmem,) * 6,
+        ) + (shape((1, heads), F32),) * 3,
+        in_specs=[hbm] * 8,
+        out_specs=(vmem,) * 8,
         scratch_shapes=[
+            pltpu.VMEM((heads, tokens), F32),
+            pltpu.VMEM((1, heads), F32),
+            pltpu.VMEM((1, heads), F32),
+            pltpu.VMEM((1, heads), F32),
             pltpu.VMEM((tokens, channels), BF16),
+            pltpu.VMEM((tokens, state), BF16),
+            pltpu.VMEM((tokens, state), BF16),
             pltpu.VMEM((tokens, channels), BF16),
-            dma((2,)),
+            dma((8,)),
             pltpu.VMEM(square, F32),
             pltpu.VMEM((8, tokens), F32),
             pltpu.VMEM((2 * tokens + 16, tokens), BF16),
@@ -415,23 +434,25 @@
             pltpu.VMEM(square, F32),
             pltpu.VMEM(square, F32),
             pltpu.VMEM(square, F32),
-            pltpu.VMEM((n, 8, tokens), F32),
-            pltpu.VMEM((steps + 1, 8, tokens), F32),
+            pltpu.VMEM((n, 1, tokens), F32),
+            pltpu.VMEM((steps + 1, 1, tokens), F32),
             dma((chunks,)), dma((chunks,)), dma((chunks,)), dma((chunks,)),
             dma((n - 1,)), dma((n - 1,)), dma((steps,)), dma((steps,)),
         ],
         compiler_params=pltpu.CompilerParams(
-            collective_id=0, has_side_effects=True, vmem_limit_bytes=60 * 2**20),
+            collective_id=0, has_side_effects=True, vmem_limit_bytes=40 * 2**20),
     )(
-        dt_raw[0].T, dt_bias[None], a_log[None], d_skip[None],
-        x_in[0], b_in[0], c_in[0], cotangent[0],
+        *(pltpu.with_memory_space_constraint(a, pltpu.HBM) for a in (
+            dt_raw[0].T, dt_bias[None], a_log[None], d_skip[None],
+            x_in[0], b_in[0], c_in[0], cotangent[0]))
     )
     out, gx, gb, gc, gdt, alog, bias, skip = pl.pallas_call(
-        functools.partial(place_outputs, heads),
-        out_shape=tuple(shape(a.shape, a.dtype) for a in made[:5]) + (shape((1, heads), F32),) * 3,
-        in_specs=[vmem] * 6,
-        out_specs=(hbm,) * 5 + (vmem,) * 3,
-        scratch_shapes=[dma((5,))],
+        functools.partial(place_outputs, 8),
+        out_shape=tuple(shape(a.shape, a.dtype) for a in made),
+        in_specs=[vmem] * 8,
+        out_specs=(hbm,) * 8,
+        scratch_shapes=[dma((8,))],
+        compiler_params=pltpu.CompilerParams(vmem_limit_bytes=4 * 2**20),
     )(*made)
     return (out[None], gx[None], gb[None], gc[None], gdt.T[None], alog[0], bias[0], skip[0])
 

time: 44.1 us -> 39.3 us (0.89)
  Pallas kernels: 43.2 us -> 38.5 us
    pallas_call x1, Pallas kernels: 40.3 us -> 37.3 us  [shards(): pl.pallas_call(functools.partial(kernel, n, m, heads, tokens), out_shape=...]
    pallas_call x1, Pallas kernels: 2.93 us -> 1.14 us  [shards(): pl.pallas_call(functools.partial(place_outputs, 8), out_shape=tuple((shap...]
where the time goes in v1:
time: 39.3 us; the launch traced here: 39.1 us
  Pallas kernels  38.5 us (98%)
  between operations  0.64 us (2%)
    pallas_call x1, Pallas kernels, shards(): pl.pallas_call(functools.partial(kernel, n, m, heads, tokens), out_shape=...  37.3 us
    pallas_call x1, Pallas kernels, shards(): pl.pallas_call(functools.partial(place_outputs, 8), out_shape=tuple((shap...  1.14 us

profile of v1, /device:TPU:0, one launch (start us, length us, event | category | flops | bytes accessed | tf_op | source)
XLA Modules:
  0.0 39.1 jit_solution(16687813042718324090)
XLA Ops:
  0.6 37.3 %shard_map.143 = (bf16[128,2560]{1,0:T(8,128)(2,1)S(1)}, bf16[128,2560]{1,0:T(8,128)(2,1)S(1)}, bf16[128,128]{1,0:T(8,128)(2,1)S(1)}, bf16[128,128]{1,0:T(8,128)...) custom-call(f32[40,128]{1,0:T(8,128)} %bitcast.24, ...), custom_call_target="tpu_custom_call" | custom-call | tf_op jit(solution)/shard_map/pallas_call | solution.py:390
  38.0 1.1 %shard_map.144 = (bf16[128,2560]{1,0:T(8,128)(2,1)}, bf16[128,2560]{1,0:T(8,128)(2,1)}, bf16[128,128]{1,0:T(8,128)(2,1)}, bf16[128,128]{1,0:T(8,128)(2,1)}, f32[...) custom-call(bf16[128,2560]{1,0:T(8,128)(2,1)S(1)} %get-tuple-element.24.refs_0_, ...), custom_call_target="tpu_custom_call" | custom-call | tf_op jit(solution)/shard_map/pallas_call | solution.py:449

commit v2 on v1

--- a/solution.py
+++ b/solution.py
@@ -10,6 +10,7 @@
 HEAD_DIM = 64
 WIDTH = 256
 LAG = 3
+UNROLL = 2
 FLAT = 64
 LOG2E = 1.4426950408889634
 F32 = jnp.float32
@@ -48,7 +49,7 @@
     dt_ref, bias_ref, alog_ref, skip_ref, x_ref, b_ref, c_ref, g_ref,
     in_sem, pad, prm, pk, apk, vt, kmod, cbm, ms, ee, we, wx, eg, sl, dc, vin, uin,
     fsend, car, bsend, ds,
-    rowa, cola, misc, dcb, gba, gca, reds, redb,
+    cum_ref, ratio, slow, rowa, cola, misc, dcb, gba, gca, reds, redb,
     fs_sem, fr_sem, bs_sem, br_sem, rs_send, rs_recv, rb_send, rb_recv,
 ):
     z = lax.axis_index("seq")
@@ -66,9 +67,14 @@
         fetch.start()
     barrier = pltpu.get_barrier_semaphore()
 
+    def wrap(place, size):
+        return jnp.where(place >= size, place - size, place)
+
+    ring_z = [wrap(z + d, n) for d in range(n)]
+    ring_w = [wrap(w + d, m) for d in range(m)]
+
     def other(d):
-        place = lax.rem(z * m + w + d, n * m)
-        return {"seq": lax.div(place, m), "batch": lax.rem(place, m)}
+        return {"seq": ring_z[d // m], "batch": ring_w[d % m]}
 
     def greet_seq(d, _):
         pl.semaphore_signal(barrier, inc=1, device_id={"seq": lax.rem(z + d, n)},
@@ -80,15 +86,12 @@
                             device_id_type=pl.DeviceIdType.MESH)
         return 0
 
-    def greet_all(d, _):
-        pl.semaphore_signal(barrier, inc=1, device_id=other(d),
-                            device_id_type=pl.DeviceIdType.MESH)
-        return 0
-
     flat = n * m <= FLAT
     peers = n * m - 1 if flat else n + m - 2
     if flat:
-        lax.fori_loop(1, n * m, greet_all, 0)
+        for d in range(1, n * m):
+            pl.semaphore_signal(barrier, inc=1, device_id=other(d),
+                                device_id_type=pl.DeviceIdType.MESH)
     else:
         lax.fori_loop(1, n, greet_seq, 0)
         lax.fori_loop(1, m, greet_batch, 0)
@@ -118,7 +121,12 @@
     rate = jnp.exp(prm[1:2, :])
     decay = jnp.where(is_head, -rate * step, 0.0)
     causal = iota(square, 0) >= iota(square, 1)
-    cum = exact(jnp.where(causal, 1.0, 0.0), decay)
+    slope = 1.0 / (1.0 + jnp.exp(-raw))
+    both_sums = exact(jnp.where(causal, 1.0, 0.0), jnp.concatenate([decay, slope], axis=1))
+    cum = both_sums[:, :tokens]
+    cum_ref[...] = cum
+    ratio[...] = slope / step
+    slow[...] = rate * both_sums[:, tokens:]
     last = cum[tokens - 1 : tokens, :]
     pk[0:tokens, :] = split3(jnp.where(is_head, jnp.exp(cum), 0.0), heads)
     pk[tokens : 2 * tokens, :] = split3(
@@ -137,12 +145,12 @@
 
     for fetch in fetches[6:]:
         fetch.wait()
-    pl.semaphore_wait(barrier, peers)
+    edge = (z == 0) | (z == n - 1)
 
     def cols(i):
         return pl.ds(pl.multiple_of(i * WIDTH, WIDTH), WIDTH)
 
-    def states(i, _):
+    def state(i):
         group = lax.shift_right_logical(iota((tokens, WIDTH), 1), 6)
         spread = jnp.where(kmod[...] - group == i * per, 1.0, 0.0).astype(BF16)
         wide = mm(pk[...], spread)
@@ -153,26 +161,35 @@
         eg_i = (g_ref[:, cols(i)].astype(F32) * wide[0:tokens]).astype(BF16)
         wx[i] = wx_i
         eg[i] = eg_i
-        sl_i = mm(bt, wx_i)
-        dc_i = mm(ct, eg_i)
-        sl[i] = sl_i
-        dc[i] = dc_i
-
-        @pl.when(z == 0)
-        def _():
-            car[i] = jnp.zeros((tokens, WIDTH), BF16)
-            fsend[i] = sl_i.astype(BF16)
-            fcopy(i).start()
-
-        @pl.when(z == n - 1)
-        def _():
-            ds[i] = jnp.zeros((tokens, WIDTH), BF16)
-            bsend[i] = dc_i.astype(BF16)
-            bcopy(i).start()
+        sl[i] = mm(bt, wx_i)
+        dc[i] = mm(ct, eg_i)
+
+    def states(k, _):
+        for u in range(UNROLL):
+            state(k * UNROLL + u)
+
+        @pl.when((k == 0) & edge)
+        def _():
+            pl.semaphore_wait(barrier, peers)
+
+        for u in range(UNROLL):
+            i = k * UNROLL + u
+
+            @pl.when(z == 0)
+            def _():
+                car[i] = jnp.zeros((tokens, WIDTH), BF16)
+                fsend[i] = sl[i].astype(BF16)
+                fcopy(i).start()
+
+            @pl.when(z == n - 1)
+            def _():
+                ds[i] = jnp.zeros((tokens, WIDTH), BF16)
+                bsend[i] = dc[i].astype(BF16)
+                bcopy(i).start()
 
         return 0
 
-    lax.fori_loop(0, chunks, states, 0)
+    lax.fori_loop(0, chunks // UNROLL, states, 0)
 
     cum2 = cum * LOG2E
     apk[...] = split3(cum2, heads)
@@ -180,6 +197,11 @@
     cbm[...] = jnp.where(causal, mm(c16, bt), 0.0)
     for acc in (rowa, cola, misc, dcb, gba, gca):
         acc[...] = jnp.zeros_like(acc)
+
+    @pl.when(jnp.logical_not(edge))
+    def _():
+        pl.semaphore_wait(barrier, peers)
+
 
     def to_heads(value, i):
         group = lax.shift_right_logical(iota((WIDTH, tokens), 0), 6)
@@ -237,6 +259,15 @@
         both = jnp.where(row == 0, d_last, 0.0) + jnp.where(row == 1, d_skip, 0.0)
         misc[...] += to_heads(both, i)
 
+    cases = set()
+    for place in range(n):
+        for j in range(chunks + LAG * max(n - 2, 0)):
+            f = j - LAG * max(place - 1, 0)
+            b = j - LAG * max(n - 2 - place, 0)
+            marks = (j < chunks, 0 <= f < chunks, 0 <= b < chunks, 0 <= min(f, b) < chunks)
+            cases.add(sum(1 << k for k, mark in enumerate(marks) if mark))
+    cases = sorted(cases - {0})
+
     def advance(j, _):
         f = j - LAG * jnp.maximum(z - 1, 0)
         b = j - LAG * jnp.maximum(n - 2 - z, 0)
@@ -262,21 +293,22 @@
             bsend[b] = (ms[b, 1:2, :] * ds[b].astype(F32) + dc[b]).astype(BF16)
             bcopy(b).start()
 
-        @pl.when(j < chunks)
-        def _():
-            within(j)
-
-        @pl.when(f_on)
-        def _():
-            forward(f)
-
-        @pl.when(b_on)
-        def _():
-            backward(b)
-
-        @pl.when((both >= 0) & (both < chunks))
-        def _():
-            sums(both)
+        kind = (
+            jnp.where(j < chunks, 1, 0) + jnp.where(f_on, 2, 0) + jnp.where(b_on, 4, 0)
+            + jnp.where((both >= 0) & (both < chunks), 8, 0)
+        )
+        for case in cases:
+
+            @pl.when(kind == case)
+            def _():
+                if case & 1:
+                    within(j)
+                if case & 2:
+                    forward(f)
+                if case & 4:
+                    backward(b)
+                if case & 8:
+                    sums(both)
 
         return 0
 
@@ -284,10 +316,8 @@
 
     d_cum = rowa[...] - cola[...]
     d_cum = d_cum + jnp.where(iota(square, 0) == tokens - 1, misc[0:1, :], 0.0)
-    later = iota(square, 0) <= iota(square, 1)
-    d_decay = exact(jnp.where(later, 1.0, 0.0), d_cum)
-    d_step = cola[...] / step - rate * d_decay
-    d_raw = d_step * (1.0 / (1.0 + jnp.exp(-raw)))
+    grad_a = jnp.sum(d_cum * cum_ref[...], axis=0, keepdims=True)
+    grad_bias = jnp.sum(cola[...] * ratio[...] - d_cum * slow[...], axis=0, keepdims=True)
 
     def turn(row, by):
         return pltpu.roll(jnp.broadcast_to(row, (8, tokens)), by, 1)[0:1, :]
@@ -296,8 +326,7 @@
         return jnp.where(head_row, row, 0.0)
 
     mine = (
-        per_head(jnp.sum(d_decay * decay, axis=0, keepdims=True))
-        + turn(per_head(jnp.sum(d_raw, axis=0, keepdims=True)), heads)
+        per_head(grad_a) + turn(per_head(grad_bias), heads)
         + turn(per_head(misc[1:2, :]), 2 * heads)
     )
 
@@ -328,10 +357,14 @@
 
     if flat:
         redb[z * m + w] = mine
-        lax.fori_loop(1, n * m, start(flat_copy), 0)
+        for d in range(1, n * m):
+            flat_copy(d).start()
     else:
         reds[z] = mine
         lax.fori_loop(1, n, start(seq_copy), 0)
+    later = iota(square, 0) <= iota(square, 1)
+    d_decay = exact(jnp.where(later, 1.0, 0.0), d_cum)
+    d_raw = cola[...] * ratio[...] - rate * slope * d_decay
     gdt_ref[...] = d_raw.T[0:heads, :]
     d_cb = jnp.where(causal, dcb[...], 0.0)
     gc_ref[...] = (gca[...] + mm(d_cb.astype(BF16), b16)).astype(BF16)
@@ -354,7 +387,8 @@
 
     lax.fori_loop(0, chunks, drain, 0)
     if flat:
-        lax.fori_loop(1, n * m, finish(flat_copy), 0)
+        for d in range(1, n * m):
+            flat_copy(d).wait()
     else:
         lax.fori_loop(1, m, finish(batch_copy), 0)
     total = jnp.sum(redb[...], axis=0)
@@ -430,6 +464,9 @@
             pltpu.VMEM(big, BF16),
             pltpu.VMEM(square, F32),
             pltpu.VMEM(square, F32),
+            pltpu.VMEM(square, F32),
+            pltpu.VMEM(square, F32),
+            pltpu.VMEM(square, F32),
             pltpu.VMEM((8, tokens), F32),
             pltpu.VMEM(square, F32),
             pltpu.VMEM(square, F32),

time: 39.3 us -> 37.3 us (0.949)
  Pallas kernels: 38.5 us -> 36.5 us
    pallas_call x1, Pallas kernels: 37.3 us -> 35.4 us  [shards(): pl.pallas_call(functools.partial(kernel, n, m, heads, tokens), out_shape=...]
where the time goes in v2:
time: 37.3 us; the launch traced here: 37.2 us
  Pallas kernels  36.5 us (98%)
  between operations  0.64 us (2%)
    pallas_call x1, Pallas kernels, shards(): pl.pallas_call(functools.partial(kernel, n, m, heads, tokens), out_shape=...  35.4 us
    pallas_call x1, Pallas kernels, shards(): pl.pallas_call(functools.partial(place_outputs, 8), out_shape=tuple((shap...  1.14 us

profile of v2, /device:TPU:0, one launch (start us, length us, event | category | flops | bytes accessed | tf_op | source)
XLA Modules:
  0.0 37.2 jit_solution(148177543986793715)
XLA Ops:
  0.6 35.4 %shard_map.143 = (bf16[128,2560]{1,0:T(8,128)(2,1)S(1)}, bf16[128,2560]{1,0:T(8,128)(2,1)S(1)}, bf16[128,128]{1,0:T(8,128)(2,1)S(1)}, bf16[128,128]{1,0:T(8,128)...) custom-call(f32[40,128]{1,0:T(8,128)} %bitcast.24, ...), custom_call_target="tpu_custom_call" | custom-call | tf_op jit(solution)/shard_map/pallas_call | solution.py:424
  36.0 1.1 %shard_map.144 = (bf16[128,2560]{1,0:T(8,128)(2,1)}, bf16[128,2560]{1,0:T(8,128)(2,1)}, bf16[128,128]{1,0:T(8,128)(2,1)}, bf16[128,128]{1,0:T(8,128)(2,1)}, f32[...) custom-call(bf16[128,2560]{1,0:T(8,128)(2,1)S(1)} %get-tuple-element.24.refs_0_, ...), custom_call_target="tpu_custom_call" | custom-call | tf_op jit(solution)/shard_map/pallas_call | solution.py:486

commit v3 on v2

--- a/solution.py
+++ b/solution.py
@@ -9,8 +9,9 @@
 
 HEAD_DIM = 64
 WIDTH = 256
-LAG = 3
-UNROLL = 2
+F_LAG = 2
+B_LAG = 3
+UNROLL = 3
 FLAT = 64
 LOG2E = 1.4426950408889634
 F32 = jnp.float32
@@ -87,8 +88,29 @@
         return 0
 
     flat = n * m <= FLAT
+    relay = flat and n > 3
     peers = n * m - 1 if flat else n + m - 2
-    if flat:
+    edge_peers = 1 if relay else peers
+    if relay:
+        @pl.when((z == 1) | (z == n - 2))
+        def _():
+            pl.semaphore_signal(
+                barrier, inc=1, device_id={"seq": jnp.where(z == 1, 0, n - 1)},
+                device_id_type=pl.DeviceIdType.MESH)
+
+        for dw in range(m):
+            for inner in range(1, n - 1):
+
+                def greet():
+                    pl.semaphore_signal(
+                        barrier, inc=1, device_id={"seq": inner, "batch": ring_w[dw]},
+                        device_id_type=pl.DeviceIdType.MESH)
+
+                if dw:
+                    greet()
+                else:
+                    pl.when(z != inner)(greet)
+    elif flat:
         for d in range(1, n * m):
             pl.semaphore_signal(barrier, inc=1, device_id=other(d),
                                 device_id_type=pl.DeviceIdType.MESH)
@@ -122,11 +144,7 @@
     decay = jnp.where(is_head, -rate * step, 0.0)
     causal = iota(square, 0) >= iota(square, 1)
     slope = 1.0 / (1.0 + jnp.exp(-raw))
-    both_sums = exact(jnp.where(causal, 1.0, 0.0), jnp.concatenate([decay, slope], axis=1))
-    cum = both_sums[:, :tokens]
-    cum_ref[...] = cum
-    ratio[...] = slope / step
-    slow[...] = rate * both_sums[:, tokens:]
+    cum = exact(jnp.where(causal, 1.0, 0.0), decay)
     last = cum[tokens - 1 : tokens, :]
     pk[0:tokens, :] = split3(jnp.where(is_head, jnp.exp(cum), 0.0), heads)
     pk[tokens : 2 * tokens, :] = split3(
@@ -146,6 +164,7 @@
     for fetch in fetches[6:]:
         fetch.wait()
     edge = (z == 0) | (z == n - 1)
+    place = z * m + w
 
     def cols(i):
         return pl.ds(pl.multiple_of(i * WIDTH, WIDTH), WIDTH)
@@ -164,33 +183,39 @@
         sl[i] = mm(bt, wx_i)
         dc[i] = mm(ct, eg_i)
 
+    def announce(i):
+        @pl.when(z == 0)
+        def _():
+            car[i] = jnp.zeros((tokens, WIDTH), BF16)
+            fsend[i] = sl[i].astype(BF16)
+            fcopy(i).start()
+
+        @pl.when(z == n - 1)
+        def _():
+            ds[i] = jnp.zeros((tokens, WIDTH), BF16)
+            bsend[i] = dc[i].astype(BF16)
+            bcopy(i).start()
+
     def states(k, _):
-        for u in range(UNROLL):
-            state(k * UNROLL + u)
-
-        @pl.when((k == 0) & edge)
-        def _():
-            pl.semaphore_wait(barrier, peers)
-
-        for u in range(UNROLL):
-            i = k * UNROLL + u
-
-            @pl.when(z == 0)
-            def _():
-                car[i] = jnp.zeros((tokens, WIDTH), BF16)
-                fsend[i] = sl[i].astype(BF16)
-                fcopy(i).start()
-
-            @pl.when(z == n - 1)
-            def _():
-                ds[i] = jnp.zeros((tokens, WIDTH), BF16)
-                bsend[i] = dc[i].astype(BF16)
-                bcopy(i).start()
-
+        for u in range(unroll):
+            state(1 + k * unroll + u)
+        for u in range(unroll):
+            announce(1 + k * unroll + u)
         return 0
 
-    lax.fori_loop(0, chunks // UNROLL, states, 0)
-
+    state(0)
+
+    @pl.when(edge)
+    def _():
+        pl.semaphore_wait(barrier, edge_peers)
+
+    announce(0)
+    unroll = UNROLL if (chunks - 1) % UNROLL == 0 else 1
+    lax.fori_loop(0, (chunks - 1) // unroll, states, 0)
+
+    cum_ref[...] = cum
+    ratio[...] = slope / step
+    slow[...] = rate * exact(jnp.where(causal, 1.0, 0.0), slope)
     cum2 = cum * LOG2E
     apk[...] = split3(cum2, heads)
     vt[...] = (cum2 - jnp.log(step) * LOG2E).T
@@ -260,17 +285,17 @@
         misc[...] += to_heads(both, i)
 
     cases = set()
-    for place in range(n):
-        for j in range(chunks + LAG * max(n - 2, 0)):
-            f = j - LAG * max(place - 1, 0)
-            b = j - LAG * max(n - 2 - place, 0)
+    for row in range(n):
+        for j in range(chunks + max(F_LAG, B_LAG) * max(n - 2, 0)):
+            f = j - F_LAG * max(row - 1, 0)
+            b = j - B_LAG * max(n - 2 - row, 0)
             marks = (j < chunks, 0 <= f < chunks, 0 <= b < chunks, 0 <= min(f, b) < chunks)
             cases.add(sum(1 << k for k, mark in enumerate(marks) if mark))
     cases = sorted(cases - {0})
 
     def advance(j, _):
-        f = j - LAG * jnp.maximum(z - 1, 0)
-        b = j - LAG * jnp.maximum(n - 2 - z, 0)
+        f = j - F_LAG * jnp.maximum(z - 1, 0)
+        b = j - B_LAG * jnp.maximum(n - 2 - z, 0)
         both = jnp.minimum(f, b)
         f_on = (f >= 0) & (f < chunks)
         b_on = (b >= 0) & (b < chunks)
@@ -312,7 +337,7 @@
 
         return 0
 
-    lax.fori_loop(0, chunks + LAG * max(n - 2, 0), advance, 0)
+    lax.fori_loop(0, chunks + max(F_LAG, B_LAG) * max(n - 2, 0), advance, 0)
 
     d_cum = rowa[...] - cola[...]
     d_cum = d_cum + jnp.where(iota(square, 0) == tokens - 1, misc[0:1, :], 0.0)
@@ -342,11 +367,18 @@
             recv_sem=rb_recv.at[d - 1], device_id={"batch": lax.rem(w + d, m)},
             device_id_type=pl.DeviceIdType.MESH)
 
-    def flat_copy(d):
-        place = z * m + w
+    def flat_copy(to):
         return pltpu.make_async_remote_copy(
-            src_ref=redb.at[place], dst_ref=redb.at[place], send_sem=rb_send.at[d - 1],
-            recv_sem=rb_recv.at[d - 1], device_id=other(d),
+            src_ref=redb.at[place], dst_ref=redb.at[place], send_sem=rb_send.at[to],
+            recv_sem=rb_recv.at[place],
+            device_id={"seq": jnp.int32(to // m), "batch": jnp.int32(to % m)},
+            device_id_type=pl.DeviceIdType.MESH)
+
+    def flat_from(source):
+        return pltpu.make_async_remote_copy(
+            src_ref=redb.at[source], dst_ref=redb.at[source], send_sem=rb_send.at[source],
+            recv_sem=rb_recv.at[source],
+            device_id={"seq": jnp.int32(source // m), "batch": jnp.int32(source % m)},
             device_id_type=pl.DeviceIdType.MESH)
 
     def start(copy):
@@ -356,9 +388,9 @@
         return lambda d, _: (copy(d).wait(), 0)[1]
 
     if flat:
-        redb[z * m + w] = mine
-        for d in range(1, n * m):
-            flat_copy(d).start()
+        redb[place] = mine
+        for to in range(n * m):
+            pl.when(place != to)(lambda: flat_copy(to).start())
     else:
         reds[z] = mine
         lax.fori_loop(1, n, start(seq_copy), 0)
@@ -387,8 +419,8 @@
 
     lax.fori_loop(0, chunks, drain, 0)
     if flat:
-        for d in range(1, n * m):
-            flat_copy(d).wait()
+        for source in range(n * m):
+            pl.when(place != source)(lambda: flat_from(source).wait())
     else:
         lax.fori_loop(1, m, finish(batch_copy), 0)
     total = jnp.sum(redb[...], axis=0)
@@ -414,7 +446,7 @@
     channels = x_in.shape[2]
     state = b_in.shape[2]
     chunks = channels // WIDTH
-    steps = n * m - 1 if n * m <= FLAT else m - 1
+    steps = n * m if n * m <= FLAT else m - 1
     big = (chunks, tokens, WIDTH)
     square = (tokens, tokens)
     vmem = pl.BlockSpec(memory_space=pltpu.VMEM)
@@ -472,7 +504,7 @@
             pltpu.VMEM(square, F32),
             pltpu.VMEM(square, F32),
             pltpu.VMEM((n, 1, tokens), F32),
-            pltpu.VMEM((steps + 1, 1, tokens), F32),
+            pltpu.VMEM((n * m if n * m <= FLAT else m, 1, tokens), F32),
             dma((chunks,)), dma((chunks,)), dma((chunks,)), dma((chunks,)),
             dma((n - 1,)), dma((n - 1,)), dma((steps,)), dma((steps,)),
         ],

time: 37.3 us -> 36 us (0.965)
  Pallas kernels: 36.5 us -> 35.3 us
    pallas_call x1, Pallas kernels: 35.4 us -> 34.1 us  [shards(): pl.pallas_call(functools.partial(kernel, n, m, heads, tokens), out_shape=...]
where the time goes in v3:
time: 36 us; the launch traced here: 35.9 us
  Pallas kernels  35.3 us (98%)
  between operations  0.64 us (2%)
    pallas_call x1, Pallas kernels, shards(): pl.pallas_call(functools.partial(kernel, n, m, heads, tokens), out_shape=...  34.1 us
    pallas_call x1, Pallas kernels, shards(): pl.pallas_call(functools.partial(place_outputs, 8), out_shape=tuple((shap...  1.14 us

profile of v3, /device:TPU:0, one launch (start us, length us, event | category | flops | bytes accessed | tf_op | source)
XLA Modules:
  0.0 35.9 jit_solution(5771011204931947611)
XLA Ops:
  0.6 34.1 %shard_map.143 = (bf16[128,2560]{1,0:T(8,128)(2,1)S(1)}, bf16[128,2560]{1,0:T(8,128)(2,1)S(1)}, bf16[128,128]{1,0:T(8,128)(2,1)S(1)}, bf16[128,128]{1,0:T(8,128)...) custom-call(f32[40,128]{1,0:T(8,128)} %bitcast.24, ...), custom_call_target="tpu_custom_call" | custom-call | tf_op jit(solution)/shard_map/pallas_call | solution.py:456
  34.8 1.1 %shard_map.144 = (bf16[128,2560]{1,0:T(8,128)(2,1)}, bf16[128,2560]{1,0:T(8,128)(2,1)}, bf16[128,128]{1,0:T(8,128)(2,1)}, bf16[128,128]{1,0:T(8,128)(2,1)}, f32[...) custom-call(bf16[128,2560]{1,0:T(8,128)(2,1)S(1)} %get-tuple-element.24.refs_0_, ...), custom_call_target="tpu_custom_call" | custom-call | tf_op jit(solution)/shard_map/pallas_call | solution.py:518

commit v4 on v3

--- a/solution.py
+++ b/solution.py
@@ -173,6 +173,7 @@
         group = lax.shift_right_logical(iota((tokens, WIDTH), 1), 6)
         spread = jnp.where(kmod[...] - group == i * per, 1.0, 0.0).astype(BF16)
         wide = mm(pk[...], spread)
+        yield
         ee[i] = wide[0:tokens]
         we[i] = wide[tokens : 2 * tokens]
         ms[i] = wide[2 * tokens : 2 * tokens + 8]
@@ -180,8 +181,17 @@
         eg_i = (g_ref[:, cols(i)].astype(F32) * wide[0:tokens]).astype(BF16)
         wx[i] = wx_i
         eg[i] = eg_i
-        sl[i] = mm(bt, wx_i)
-        dc[i] = mm(ct, eg_i)
+        yield
+        sl_i = mm(bt, wx_i)
+        dc_i = mm(ct, eg_i)
+        yield
+        sl[i] = sl_i
+        dc[i] = dc_i
+
+    def together(*stages):
+        stages = list(stages)
+        while stages:
+            stages = [stage for stage in stages if next(stage, 0) is None]
 
     def announce(i):
         @pl.when(z == 0)
@@ -197,13 +207,12 @@
             bcopy(i).start()
 
     def states(k, _):
-        for u in range(unroll):
-            state(1 + k * unroll + u)
+        together(*(state(1 + k * unroll + u) for u in range(unroll)))
         for u in range(unroll):
             announce(1 + k * unroll + u)
         return 0
 
-    state(0)
+    together(state(0))
 
     @pl.when(edge)
     def _():
@@ -241,39 +250,62 @@
         right = jnp.where(lane < HEAD_DIM, 0.0, 1.0).astype(BF16)
         second = jnp.where(iota((tokens, 2 * tokens), 1) < tokens, 0, 1)
         table = kmod[:, 0:1] - second
-        cb2 = jnp.concatenate([cbm[...], cbm[...]], axis=1)
-        for q in range(WIDTH // 128):
-            head = i * per + 2 * q
-            pair = pl.ds(pl.multiple_of(i * WIDTH + q * 128, 128), 128)
-            xq = x_ref[:, pair]
-            gq = g_ref[:, pair]
-            xs = jnp.concatenate([xq * left, xq * right], axis=0)
-            gs = jnp.concatenate([gq * left, gq * right], axis=0)
-            pick = jnp.where(table == head, 1.0, 0.0).astype(BF16)
+        count = WIDTH // 128
+        heads_of = [i * per + 2 * q for q in range(count)]
+        pairs = [pl.ds(pl.multiple_of(i * WIDTH + q * 128, 128), 128) for q in range(count)]
+        xqs = [x_ref[:, pair] for pair in pairs]
+        gqs = [g_ref[:, pair] for pair in pairs]
+        xss = [jnp.concatenate([xq * left, xq * right], axis=0) for xq in xqs]
+        gss = [jnp.concatenate([gq * left, gq * right], axis=0) for gq in gqs]
+        logs = [
+            mm(apk[...], jnp.where(table == head, 1.0, 0.0).astype(BF16)) for head in heads_of]
+        gates = []
+        for head, log in zip(heads_of, logs):
             v_row = jnp.concatenate([vt[pl.ds(head, 1), :], vt[pl.ds(head + 1, 1), :]], axis=1)
-            gate = jnp.exp2(jnp.minimum(mm(apk[...], pick) - v_row, 100.0))
-            scores = (gate * cb2).astype(BF16)
-            vin[i, :, q * 128 : (q + 1) * 128] = mm(scores, xs)
-            turned = jnp.concatenate([scores[:, :tokens].T, scores[:, tokens:].T], axis=1)
-            uin[i, :, q * 128 : (q + 1) * 128] = mm(turned, gs)
-            d_gate = mm_nt(gq, xs) * gate
-            dcb[...] += d_gate[:, :tokens] + d_gate[:, tokens:]
+            gates.append(jnp.exp2(jnp.minimum(log - v_row, 100.0)))
+        cb = cbm[...]
+        scores = [
+            [(gate[:, h * tokens : (h + 1) * tokens] * cb).astype(BF16) for h in range(2)]
+            for gate in gates]
+        turned = [jnp.concatenate([part.T for part in both], axis=1) for both in scores]
+        grads = [mm_nt(gq, xs) * gate for gq, xs, gate in zip(gqs, xss, gates)]
+        for q in range(count):
+            vin[i, :, q * 128 : (q + 1) * 128] = mm(jnp.concatenate(scores[q], axis=1), xss[q])
+            uin[i, :, q * 128 : (q + 1) * 128] = mm(turned[q], gss[q])
+        total = grads[0][:, :tokens] + grads[0][:, tokens:]
+        for grad in grads[1:]:
+            total = total + grad[:, :tokens] + grad[:, tokens:]
+        dcb[...] += total
 
     def forward(i):
+        state_in = car[i]
+        inter = mm(c16, state_in)
+        to_c = mm_nt(eg[i], state_in)
+        yield
         x_i = x_ref[:, cols(i)].astype(F32)
-        v = vin[i] + ee[i] * mm(c16, car[i])
+        v = vin[i] + ee[i] * inter
         out_ref[:, cols(i)] = (v + ms[i, 0:1, :] * x_i).astype(BF16)
-        rowa[...] += to_heads(g_ref[:, cols(i)].astype(F32) * v, i)
-        gca[...] += mm_nt(eg[i], car[i])
+        share = g_ref[:, cols(i)].astype(F32) * v
+        yield
+        share = to_heads(share, i)
+        yield
+        rowa[...] += share
+        gca[...] += to_c
 
     def backward(i):
+        state_in = ds[i]
+        from_state = mm(b16, state_in)
+        to_b = mm_nt(wx[i], state_in)
+        yield
         g_i = g_ref[:, cols(i)].astype(F32)
         u = uin[i]
-        from_state = mm(b16, ds[i])
         gx_ref[:, cols(i)] = (u + we[i] * from_state + ms[i, 0:1, :] * g_i).astype(BF16)
         share = x_ref[:, cols(i)].astype(F32) * u + wx[i].astype(F32) * from_state
-        cola[...] += to_heads(share, i)
-        gba[...] += mm_nt(wx[i], ds[i])
+        yield
+        share = to_heads(share, i)
+        yield
+        cola[...] += share
+        gba[...] += to_b
 
     def sums(i):
         onward = ms[i, 1:2, :] * car[i].astype(F32) + sl[i]
@@ -282,14 +314,17 @@
             g_ref[:, cols(i)].astype(F32) * x_ref[:, cols(i)].astype(F32), axis=0, keepdims=True)
         row = iota((8, WIDTH), 0)
         both = jnp.where(row == 0, d_last, 0.0) + jnp.where(row == 1, d_skip, 0.0)
-        misc[...] += to_heads(both, i)
+        yield
+        both = to_heads(both, i)
+        yield
+        misc[...] += both
 
     cases = set()
     for row in range(n):
         for j in range(chunks + max(F_LAG, B_LAG) * max(n - 2, 0)):
             f = j - F_LAG * max(row - 1, 0)
             b = j - B_LAG * max(n - 2 - row, 0)
-            marks = (j < chunks, 0 <= f < chunks, 0 <= b < chunks, 0 <= min(f, b) < chunks)
+            marks = (0 <= f < chunks, 0 <= b < chunks, 0 <= min(f, b) < chunks)
             cases.add(sum(1 << k for k, mark in enumerate(marks) if mark))
     cases = sorted(cases - {0})
 
@@ -309,6 +344,10 @@
         def _():
             fcopy(f).start()
 
+        @pl.when(j < chunks)
+        def _():
+            within(j)
+
         @pl.when(b_on & (z < n - 1))
         def _():
             bcopy(b).wait_recv()
@@ -319,21 +358,16 @@
             bcopy(b).start()
 
         kind = (
-            jnp.where(j < chunks, 1, 0) + jnp.where(f_on, 2, 0) + jnp.where(b_on, 4, 0)
-            + jnp.where((both >= 0) & (both < chunks), 8, 0)
+            jnp.where(f_on, 1, 0) + jnp.where(b_on, 2, 0)
+            + jnp.where((both >= 0) & (both < chunks), 4, 0)
         )
         for case in cases:
 
             @pl.when(kind == case)
             def _():
-                if case & 1:
-                    within(j)
-                if case & 2:
-                    forward(f)
-                if case & 4:
-                    backward(b)
-                if case & 8:
-                    sums(both)
+                together(*(
+                    part(i) for bit, part, i in ((1, forward, f), (2, backward, b), (4, sums, both))
+                    if case & bit))
 
         return 0
 

time: 36 us -> 35.3 us (0.981)
  Pallas kernels: 35.3 us -> 34.5 us
    pallas_call x1, Pallas kernels: 34.1 us -> 33.4 us  [shards(): pl.pallas_call(functools.partial(kernel, n, m, heads, tokens), out_shape=...]
where the time goes in v4:
time: 35.3 us; the launch traced here: 35.2 us
  Pallas kernels  34.5 us (98%)
  between operations  0.64 us (2%)
    pallas_call x1, Pallas kernels, shards(): pl.pallas_call(functools.partial(kernel, n, m, heads, tokens), out_shape=...  33.4 us
    pallas_call x1, Pallas kernels, shards(): pl.pallas_call(functools.partial(place_outputs, 8), out_shape=tuple((shap...  1.14 us

profile of v4, /device:TPU:0, one launch (start us, length us, event | category | flops | bytes accessed | tf_op | source)
XLA Modules:
  0.0 35.2 jit_solution(3411364476488791273)
XLA Ops:
  0.6 33.4 %shard_map.143 = (bf16[128,2560]{1,0:T(8,128)(2,1)S(1)}, bf16[128,2560]{1,0:T(8,128)(2,1)S(1)}, bf16[128,128]{1,0:T(8,128)(2,1)S(1)}, bf16[128,128]{1,0:T(8,128)...) custom-call(f32[40,128]{1,0:T(8,128)} %bitcast.24, ...), custom_call_target="tpu_custom_call" | custom-call | tf_op jit(solution)/shard_map/pallas_call | solution.py:490
  34.0 1.1 %shard_map.144 = (bf16[128,2560]{1,0:T(8,128)(2,1)}, bf16[128,2560]{1,0:T(8,128)(2,1)}, bf16[128,128]{1,0:T(8,128)(2,1)}, bf16[128,128]{1,0:T(8,128)(2,1)}, f32[...) custom-call(bf16[128,2560]{1,0:T(8,128)(2,1)S(1)} %get-tuple-element.24.refs_0_, ...), custom_call_target="tpu_custom_call" | custom-call | tf_op jit(solution)/shard_map/pallas_call | solution.py:552

commit v5 on v4

--- a/solution.py
+++ b/solution.py
@@ -48,7 +48,7 @@
     dt_hbm, bias_hbm, alog_hbm, skip_hbm, x_hbm, b_hbm, c_hbm, g_hbm,
     out_ref, gx_ref, gb_ref, gc_ref, gdt_ref, ga_out, gbias_out, gskip_out,
     dt_ref, bias_ref, alog_ref, skip_ref, x_ref, b_ref, c_ref, g_ref,
-    in_sem, pad, prm, pk, apk, vt, kmod, cbm, ms, ee, we, wx, eg, sl, dc, vin, uin,
+    in_sem, x_sem, g_sem, pad, prm, pk, apk, vt, kmod, cbm, ms, ee, we, wx, eg, sl, dc, vin, uin,
     fsend, car, bsend, ds,
     cum_ref, ratio, slow, rowa, cola, misc, dcb, gba, gca, reds, redb,
     fs_sem, fr_sem, bs_sem, br_sem, rs_send, rs_recv, rb_send, rb_recv,
@@ -58,14 +58,30 @@
     chunks = heads * HEAD_DIM // WIDTH
     per = WIDTH // HEAD_DIM
 
-    fetches = [
+    unroll = UNROLL if (chunks - 1) % UNROLL == 0 else 1
+    groups = 1 + (chunks - 1) // unroll
+    small = [
         pltpu.make_async_copy(a, b, in_sem.at[i])
         for i, (a, b) in enumerate((
             (dt_hbm, dt_ref), (bias_hbm, bias_ref), (alog_hbm, alog_ref), (skip_hbm, skip_ref),
-            (b_hbm, b_ref), (c_hbm, c_ref), (x_hbm, x_ref), (g_hbm, g_ref)))
+            (b_hbm, b_ref), (c_hbm, c_ref)))
     ]
-    for fetch in fetches:
-        fetch.start()
+
+    def fetch(k, first):
+        size = WIDTH if first else unroll * WIDTH
+        low = 0 if first else pl.multiple_of(WIDTH + (k - 1) * unroll * WIDTH, WIDTH)
+        part = pl.ds(low, size)
+        return (
+            pltpu.make_async_copy(x_hbm.at[:, part], x_ref.at[:, part], x_sem.at[k]),
+            pltpu.make_async_copy(g_hbm.at[:, part], g_ref.at[:, part], g_sem.at[k]),
+        )
+
+    def fetch_small():
+        for copy in small:
+            copy.start()
+        for copy in fetch(0, True):
+            copy.start()
+
     barrier = pltpu.get_barrier_semaphore()
 
     def wrap(place, size):
@@ -91,6 +107,8 @@
     relay = flat and n > 3
     peers = n * m - 1 if flat else n + m - 2
     edge_peers = 1 if relay else peers
+    if not relay:
+        fetch_small()
     if relay:
         @pl.when((z == 1) | (z == n - 2))
         def _():
@@ -98,6 +116,7 @@
                 barrier, inc=1, device_id={"seq": jnp.where(z == 1, 0, n - 1)},
                 device_id_type=pl.DeviceIdType.MESH)
 
+        fetch_small()
         for dw in range(m):
             for inner in range(1, n - 1):
 
@@ -118,20 +137,24 @@
         lax.fori_loop(1, n, greet_seq, 0)
         lax.fori_loop(1, m, greet_batch, 0)
 
+    for k in range(1, groups):
+        for copy in fetch(k, False):
+            copy.start()
+
     def fcopy(i):
         return pltpu.make_async_remote_copy(
-            src_ref=fsend.at[i], dst_ref=car.at[i], send_sem=fs_sem.at[i], recv_sem=fr_sem.at[i],
+            src_ref=fsend.at[i], dst_ref=car.at[i], send_sem=fs_sem.at[0], recv_sem=fr_sem.at[i],
             device_id={"seq": jnp.minimum(z + 1, n - 1)}, device_id_type=pl.DeviceIdType.MESH)
 
     def bcopy(i):
         return pltpu.make_async_remote_copy(
-            src_ref=bsend.at[i], dst_ref=ds.at[i], send_sem=bs_sem.at[i], recv_sem=br_sem.at[i],
+            src_ref=bsend.at[i], dst_ref=ds.at[i], send_sem=bs_sem.at[0], recv_sem=br_sem.at[i],
             device_id={"seq": jnp.maximum(z - 1, 0)}, device_id_type=pl.DeviceIdType.MESH)
 
     pad[...] = jnp.zeros_like(pad)
     prm[...] = jnp.zeros_like(prm)
-    for fetch in fetches[:6]:
-        fetch.wait()
+    for copy in small:
+        copy.wait()
     pad[0:heads, :] = dt_ref[...]
     prm[0:1, :heads] = bias_ref[...]
     prm[1:2, :heads] = alog_ref[...]
@@ -161,8 +184,6 @@
     bt = b16.astype(F32).T.astype(BF16)
     ct = c16.astype(F32).T.astype(BF16)
 
-    for fetch in fetches[6:]:
-        fetch.wait()
     edge = (z == 0) | (z == n - 1)
     place = z * m + w
 
@@ -207,11 +228,15 @@
             bcopy(i).start()
 
     def states(k, _):
+        for copy in fetch(1 + k, False):
+            copy.wait()
         together(*(state(1 + k * unroll + u) for u in range(unroll)))
         for u in range(unroll):
             announce(1 + k * unroll + u)
         return 0
 
+    for copy in fetch(0, True):
+        copy.wait()
     together(state(0))
 
     @pl.when(edge)
@@ -219,7 +244,6 @@
         pl.semaphore_wait(barrier, edge_peers)
 
     announce(0)
-    unroll = UNROLL if (chunks - 1) % UNROLL == 0 else 1
     lax.fori_loop(0, (chunks - 1) // unroll, states, 0)
 
     cum_ref[...] = cum
@@ -403,17 +427,14 @@
 
     def flat_copy(to):
         return pltpu.make_async_remote_copy(
-            src_ref=redb.at[place], dst_ref=redb.at[place], send_sem=rb_send.at[to],
-            recv_sem=rb_recv.at[place],
+            src_ref=redb.at[place], dst_ref=redb.at[place], send_sem=rb_send.at[0],
+            recv_sem=rb_recv.at[0],
             device_id={"seq": jnp.int32(to // m), "batch": jnp.int32(to % m)},
             device_id_type=pl.DeviceIdType.MESH)
 
-    def flat_from(source):
-        return pltpu.make_async_remote_copy(
-            src_ref=redb.at[source], dst_ref=redb.at[source], send_sem=rb_send.at[source],
-            recv_sem=rb_recv.at[source],
-            device_id={"seq": jnp.int32(source // m), "batch": jnp.int32(source % m)},
-            device_id_type=pl.DeviceIdType.MESH)
+    def flat_wait(sem):
+        rows = redb.at[pl.ds(0, n * m - 1)]
+        pltpu.make_async_copy(rows, rows, sem).wait()
 
     def start(copy):
         return lambda d, _: (copy(d).start(), 0)[1]
@@ -440,21 +461,17 @@
         redb[w] = lax.fori_loop(0, n, lambda i, t: t + reds[i], jnp.zeros((1, tokens), F32))
         lax.fori_loop(1, m, start(batch_copy), 0)
 
-    def drain(i, _):
-        @pl.when(z < n - 1)
-        def _():
-            fcopy(i).wait_send()
-
-        @pl.when(z > 0)
-        def _():
-            bcopy(i).wait_send()
-
-        return 0
-
-    lax.fori_loop(0, chunks, drain, 0)
+    @pl.when(z < n - 1)
+    def _():
+        pltpu.make_async_copy(fsend, fsend, fs_sem.at[0]).wait()
+
+    @pl.when(z > 0)
+    def _():
+        pltpu.make_async_copy(bsend, bsend, bs_sem.at[0]).wait()
+
     if flat:
-        for source in range(n * m):
-            pl.when(place != source)(lambda: flat_from(source).wait())
+        flat_wait(rb_send.at[0])
+        flat_wait(rb_recv.at[0])
     else:
         lax.fori_loop(1, m, finish(batch_copy), 0)
     total = jnp.sum(redb[...], axis=0)
@@ -480,7 +497,9 @@
     channels = x_in.shape[2]
     state = b_in.shape[2]
     chunks = channels // WIDTH
-    steps = n * m if n * m <= FLAT else m - 1
+    steps = 1 if n * m <= FLAT else m - 1
+    stops = 1 if n * m <= FLAT else n - 1
+    groups = 1 + (chunks - 1) // (UNROLL if (chunks - 1) % UNROLL == 0 else 1)
     big = (chunks, tokens, WIDTH)
     square = (tokens, tokens)
     vmem = pl.BlockSpec(memory_space=pltpu.VMEM)
@@ -507,7 +526,7 @@
             pltpu.VMEM((tokens, state), BF16),
             pltpu.VMEM((tokens, state), BF16),
             pltpu.VMEM((tokens, channels), BF16),
-            dma((8,)),
+            dma((6,)), dma((groups,)), dma((groups,)),
             pltpu.VMEM(square, F32),
             pltpu.VMEM((8, tokens), F32),
             pltpu.VMEM((2 * tokens + 16, tokens), BF16),
@@ -539,8 +558,8 @@
             pltpu.VMEM(square, F32),
             pltpu.VMEM((n, 1, tokens), F32),
             pltpu.VMEM((n * m if n * m <= FLAT else m, 1, tokens), F32),
-            dma((chunks,)), dma((chunks,)), dma((chunks,)), dma((chunks,)),
-            dma((n - 1,)), dma((n - 1,)), dma((steps,)), dma((steps,)),
+            dma((1,)), dma((chunks,)), dma((1,)), dma((chunks,)),
+            dma((stops,)), dma((stops,)), dma((steps,)), dma((steps,)),
         ],
         compiler_params=pltpu.CompilerParams(
             collective_id=0, has_side_effects=True, vmem_limit_bytes=40 * 2**20),

time: 35.3 us -> 34.6 us (0.980)
  Pallas kernels: 34.5 us -> 33.8 us
    pallas_call x1, Pallas kernels: 33.4 us -> 32.7 us  [shards(): pl.pallas_call(functools.partial(kernel, n, m, heads, tokens), out_shape=...]
where the time goes in v5:
time: 34.6 us; the launch traced here: 34.5 us
  Pallas kernels  33.8 us (98%)
  between operations  0.64 us (2%)
    pallas_call x1, Pallas kernels, shards(): pl.pallas_call(functools.partial(kernel, n, m, heads, tokens), out_shape=...  32.7 us
    pallas_call x1, Pallas kernels, shards(): pl.pallas_call(functools.partial(place_outputs, 8), out_shape=tuple((shap...  1.14 us

profile of v5, /device:TPU:0, one launch (start us, length us, event | category | flops | bytes accessed | tf_op | source)
XLA Modules:
  0.0 34.5 jit_solution(6917335849871138830)
XLA Ops:
  0.6 32.7 %shard_map.143 = (bf16[128,2560]{1,0:T(8,128)(2,1)S(1)}, bf16[128,2560]{1,0:T(8,128)(2,1)S(1)}, bf16[128,128]{1,0:T(8,128)(2,1)S(1)}, bf16[128,128]{1,0:T(8,128)...) custom-call(f32[40,128]{1,0:T(8,128)} %bitcast.24, ...), custom_call_target="tpu_custom_call" | custom-call | tf_op jit(solution)/shard_map/pallas_call | solution.py:509
  33.3 1.1 %shard_map.144 = (bf16[128,2560]{1,0:T(8,128)(2,1)}, bf16[128,2560]{1,0:T(8,128)(2,1)}, bf16[128,128]{1,0:T(8,128)(2,1)}, bf16[128,128]{1,0:T(8,128)(2,1)}, f32[...) custom-call(bf16[128,2560]{1,0:T(8,128)(2,1)S(1)} %get-tuple-element.24.refs_0_, ...), custom_call_target="tpu_custom_call" | custom-call | tf_op jit(solution)/shard_map/pallas_call | solution.py:571

commit v6 on v5

--- a/solution.py
+++ b/solution.py
@@ -51,7 +51,7 @@
     in_sem, x_sem, g_sem, pad, prm, pk, apk, vt, kmod, cbm, ms, ee, we, wx, eg, sl, dc, vin, uin,
     fsend, car, bsend, ds,
     cum_ref, ratio, slow, rowa, cola, misc, dcb, gba, gca, reds, redb,
-    fs_sem, fr_sem, bs_sem, br_sem, rs_send, rs_recv, rb_send, rb_recv,
+    fs_sem, fr_sem, bs_sem, br_sem, rs_sems, rb_send, rb_recv,
 ):
     z = lax.axis_index("seq")
     w = lax.axis_index("batch")
@@ -415,8 +415,8 @@
 
     def seq_copy(d):
         return pltpu.make_async_remote_copy(
-            src_ref=reds.at[z], dst_ref=reds.at[z], send_sem=rs_send.at[d - 1],
-            recv_sem=rs_recv.at[d - 1], device_id={"seq": lax.rem(z + d, n)},
+            src_ref=reds.at[z], dst_ref=reds.at[z], send_sem=rs_sems.at[d - 1],
+            recv_sem=rs_sems.at[n - 1 + d - 1], device_id={"seq": lax.rem(z + d, n)},
             device_id_type=pl.DeviceIdType.MESH)
 
     def batch_copy(d):
@@ -498,7 +498,7 @@
     state = b_in.shape[2]
     chunks = channels // WIDTH
     steps = 1 if n * m <= FLAT else m - 1
-    stops = 1 if n * m <= FLAT else n - 1
+    stops = 1 if n * m <= FLAT else 2 * (n - 1)
     groups = 1 + (chunks - 1) // (UNROLL if (chunks - 1) % UNROLL == 0 else 1)
     big = (chunks, tokens, WIDTH)
     square = (tokens, tokens)
@@ -559,7 +559,7 @@
             pltpu.VMEM((n, 1, tokens), F32),
             pltpu.VMEM((n * m if n * m <= FLAT else m, 1, tokens), F32),
             dma((1,)), dma((chunks,)), dma((1,)), dma((chunks,)),
-            dma((stops,)), dma((stops,)), dma((steps,)), dma((steps,)),
+            dma((stops,)), dma((steps,)), dma((steps,)),
         ],
         compiler_params=pltpu.CompilerParams(
             collective_id=0, has_side_effects=True, vmem_limit_bytes=40 * 2**20),

time: 34.6 us -> 34.6 us (level)
  no operation moved by 1% of the time
where the time goes in v6:
time: 34.6 us; the launch traced here: 34.5 us
  Pallas kernels  33.8 us (98%)
  between operations  0.64 us (2%)
    pallas_call x1, Pallas kernels, shards(): pl.pallas_call(functools.partial(kernel, n, m, heads, tokens), out_shape=...  32.7 us
    pallas_call x1, Pallas kernels, shards(): pl.pallas_call(functools.partial(place_outputs, 8), out_shape=tuple((shap...  1.14 us

profile of v6, /device:TPU:0, one launch (start us, length us, event | category | flops | bytes accessed | tf_op | source)
XLA Modules:
  0.0 34.5 jit_solution(13989757052160672960)
XLA Ops:
  0.6 32.7 %shard_map.143 = (bf16[128,2560]{1,0:T(8,128)(2,1)S(1)}, bf16[128,2560]{1,0:T(8,128)(2,1)S(1)}, bf16[128,128]{1,0:T(8,128)(2,1)S(1)}, bf16[128,128]{1,0:T(8,128)...) custom-call(f32[40,128]{1,0:T(8,128)} %bitcast.24, ...), custom_call_target="tpu_custom_call" | custom-call | tf_op jit(solution)/shard_map/pallas_call | solution.py:509
  33.3 1.1 %shard_map.144 = (bf16[128,2560]{1,0:T(8,128)(2,1)}, bf16[128,2560]{1,0:T(8,128)(2,1)}, bf16[128,128]{1,0:T(8,128)(2,1)}, bf16[128,128]{1,0:T(8,128)(2,1)}, f32[...) custom-call(bf16[128,2560]{1,0:T(8,128)(2,1)S(1)} %get-tuple-element.24.refs_0_, ...), custom_call_target="tpu_custom_call" | custom-call | tf_op jit(solution)/shard_map/pallas_call | solution.py:571

commit v7 on v6

--- a/solution.py
+++ b/solution.py
@@ -483,7 +483,7 @@
 def place_outputs(count, *refs):
     sems = refs[2 * count]
     copies = [
-        pltpu.make_async_copy(refs[i], refs[count + i], sems.at[i]) for i in range(count)
+        pltpu.make_async_copy(refs[i], refs[count + i], sems.at[0]) for i in range(count)
     ]
     for copy in copies:
         copy.start()
@@ -573,7 +573,7 @@
         out_shape=tuple(shape(a.shape, a.dtype) for a in made),
         in_specs=[vmem] * 8,
         out_specs=(hbm,) * 8,
-        scratch_shapes=[dma((8,))],
+        scratch_shapes=[dma((1,))],
         compiler_params=pltpu.CompilerParams(vmem_limit_bytes=4 * 2**20),
     )(*made)
     return (out[None], gx[None], gb[None], gc[None], gdt.T[None], alog[0], bias[0], skip[0])

time: 34.6 us -> 34.5 us (level)
  no operation moved by 1% of the time
where the time goes in v7:
time: 34.5 us; the launch traced here: 34.4 us
  Pallas kernels  33.7 us (98%)
  between operations  0.64 us (2%)
    pallas_call x1, Pallas kernels, shards(): pl.pallas_call(functools.partial(kernel, n, m, heads, tokens), out_shape=...  32.7 us
    pallas_call x1, Pallas kernels, shards(): pl.pallas_call(functools.partial(place_outputs, 8), out_shape=tuple((shap...  1.07 us

profile of v7, /device:TPU:0, one launch (start us, length us, event | category | flops | bytes accessed | tf_op | source)
XLA Modules:
  0.0 34.4 jit_solution(13516857680789725796)
XLA Ops:
  0.6 32.7 %shard_map.143 = (bf16[128,2560]{1,0:T(8,128)(2,1)S(1)}, bf16[128,2560]{1,0:T(8,128)(2,1)S(1)}, bf16[128,128]{1,0:T(8,128)(2,1)S(1)}, bf16[128,128]{1,0:T(8,128)...) custom-call(f32[40,128]{1,0:T(8,128)} %bitcast.24, ...), custom_call_target="tpu_custom_call" | custom-call | tf_op jit(solution)/shard_map/pallas_call | solution.py:509
  33.3 1.1 %shard_map.144 = (bf16[128,2560]{1,0:T(8,128)(2,1)}, bf16[128,2560]{1,0:T(8,128)(2,1)}, bf16[128,128]{1,0:T(8,128)(2,1)}, bf16[128,128]{1,0:T(8,128)(2,1)}, f32[...) custom-call(bf16[128,2560]{1,0:T(8,128)(2,1)S(1)} %get-tuple-element.24.refs_0_, ...), custom_call_target="tpu_custom_call" | custom-call | tf_op jit(solution)/shard_map/pallas_call | solution.py:571
